TPU v7x, 32 devices: a whole 2x2x4 slice. The times are simulated.
32 devices in a mesh: frame: 4 (over x, core), band: 8 (over z, y).
Axes of the slice: x: 2, y: 2, z: 4, core: 2. Of those that a mesh axis runs over, the one named last changes fastest.
Arguments:
- noisy_snapshot_stack: bfloat16 [4, 8, 180, 512], P('frame', 'band'), may hold values from -6 to 6
- gaussian_perturbation: bfloat16 [4, 8, 180, 512], P('frame', 'band'), may hold values from -6 to 6
- snapshot_noise_indices: int32 [4], P('frame'), may hold values from 0 to 3, each once
- partition_longitude_starts: int32 [4], P('frame'), may hold values from 0 to 59
- latitude_patch_tally: int32 [8], replicated, may hold values from 90 to 180
- normalizer_scaling: float32 [512], replicated, may hold values from 0.1 to 1.9
- head_score_scales: float32 [2, 8], replicated, may hold values from 0.5 to 100
- local_projection_matrices: bfloat16 [512, 1536], P(None, 'band'), may hold values from -0.25 to 0.25
- time_projection_matrices: bfloat16 [512, 1536], P(None, 'band'), may hold values from -0.25 to 0.25
- final_projection_matrices: bfloat16 [1024, 512], P(None, 'band'), may hold values from -0.1875 to 0.1875
Outputs:
- next_state: bfloat16 [4, 8, 180, 512], P('frame', 'band')
Inputs may be any that keep to these rules, and one draw needn't show every extreme that they name: `snapshot_noise_indices`: each level index 0 to 3 belongs to exactly one frame.
All inputs are finite; a program needn't handle non-finite values.
Results may differ from a plain program's by a relative error of at most 0.0071.
Values may be sent and summed in bfloat16 or wider, within the bound.
No kernel may reach another device: no remote copies, remote signals or barrier semaphores. Data moves between devices by JAX's collectives and lax.ppermute only.
A program may use at most 64 MiB of HBM per device.

v0:
```python
import math
import jax
import jax.numpy as jnp
from jax import lax
from jax.sharding import PartitionSpec as P

HEADS = 8
HEAD_DIM = 64
WINDOW = 60
PRIOR_SNAPSHOTS = 3
epsilon = 1e-06
sigma_low = 0.1
sigma_high = 2.0
keep_share = 0.8
fresh_share = 0.6


def extended(cells, sides, width):
    for axis, dim in sides:
        count = lax.axis_size(axis)
        ends = count - 1
        head = lax.slice_in_dim(cells, 0, width, axis=dim)
        tail = lax.slice_in_dim(cells, cells.shape[dim] - width, cells.shape[dim], axis=dim)
        cells = jnp.concatenate(
            [
                lax.ppermute(tail, axis, [(i, (i + 1) % count) for i in range(ends)]),
                cells,
                lax.ppermute(head, axis, [((i + 1) % count, i) for i in range(ends)]),
            ],
            axis=dim,
        )
    return cells


def shifted(block, axis, distance):
    devices = range(lax.axis_size(axis))
    route = [(i - distance, i) for i in devices if i - distance in devices]
    return lax.ppermute(block, axis, route)


def sigma_of(level, total_levels):
    return sigma_low * jnp.power(
        sigma_high / sigma_low, (level.astype(jnp.float32) + 1.0) / total_levels
    )


def unit_heads(content_vectors):
    shaped = content_vectors.reshape(content_vectors.shape[:-1] + (HEADS, HEAD_DIM))
    scale = lax.rsqrt(jnp.mean(shaped * shaped, axis=-1, keepdims=True) + epsilon)
    return (shaped * scale).reshape(content_vectors.shape)


def pick(table, index):
    return jnp.sum(jnp.where(jnp.arange(table.shape[0]) == index, table, 0))


def with_past(local, frame_dim, shifter):
    frames = local.shape[frame_dim]
    hops = -(-PRIOR_SNAPSHOTS // frames)
    pieces = [shifter(local, hop) for hop in range(hops, 0, -1)]
    joined = jnp.concatenate(pieces + [local], axis=frame_dim)
    return joined


def local_patch_mixer(
    asking_vectors,
    fringe_lookup_vectors,
    fringe_content_vectors,
    fringe_present_flags,
    snapshot_longitude_shift,
    temper,
):
    rows, lon, token_extent = asking_vectors.shape
    wins = lon // WINDOW
    asking_vectors = jnp.roll(asking_vectors, -snapshot_longitude_shift, axis=1).reshape(
        rows, wins, WINDOW, HEADS, HEAD_DIM
    )
    fringe_lookup_vectors = jnp.roll(
        fringe_lookup_vectors, -snapshot_longitude_shift, axis=1
    ).reshape(rows + 2, wins, WINDOW, HEADS, HEAD_DIM)
    fringe_content_vectors = jnp.roll(
        fringe_content_vectors, -snapshot_longitude_shift, axis=1
    ).reshape(rows + 2, wins, WINDOW, HEADS, HEAD_DIM)
    fringe_present_flags = jnp.roll(
        fringe_present_flags, -snapshot_longitude_shift, axis=1
    ).reshape(rows + 2, wins, WINDOW)
    lookup_vectors = jnp.concatenate(
        [fringe_lookup_vectors[:-2], fringe_lookup_vectors[1:-1], fringe_lookup_vectors[2:]], axis=2
    )
    content_vectors = jnp.concatenate(
        [fringe_content_vectors[:-2], fringe_content_vectors[1:-1], fringe_content_vectors[2:]],
        axis=2,
    )
    permitted_mask = jnp.concatenate(
        [fringe_present_flags[:-2], fringe_present_flags[1:-1], fringe_present_flags[2:]], axis=2
    )
    inner = jnp.arange(WINDOW)
    middle = jnp.arange(3 * WINDOW)
    itself = middle[None, :] == inner[:, None] + WINDOW
    permitted_mask = permitted_mask[:, :, None, None, :] | itself[None, None, None]
    scores = jnp.einsum(
        "rwqhd,rwkhd->rwhqk", asking_vectors, lookup_vectors, preferred_element_type=jnp.float32
    )
    scores = scores * (temper / math.sqrt(HEAD_DIM))[None, None, :, None, None]
    top = jnp.max(jnp.where(permitted_mask, scores, -jnp.inf), axis=-1, keepdims=True)
    weights = jnp.where(permitted_mask, jnp.exp(scores - top), 0.0)
    probs = (weights / jnp.sum(weights, axis=-1, keepdims=True)).astype(jnp.bfloat16)
    combined_result_field = jnp.einsum(
        "rwhqk,rwkhd->rwqhd", probs, content_vectors, preferred_element_type=jnp.float32
    )
    combined_result_field = combined_result_field.reshape(rows, lon, token_extent)
    return jnp.roll(combined_result_field, snapshot_longitude_shift, axis=1).astype(jnp.bfloat16)


def across_time_mixer(asking_vectors, lookup_vectors, content_vectors, permitted_mask, temper):
    count, token_extent = asking_vectors.shape
    span = lookup_vectors.shape[0]
    query_heads = asking_vectors.reshape(count, HEADS, HEAD_DIM)
    key_heads = lookup_vectors.reshape(span, count, HEADS, HEAD_DIM)
    value_heads = content_vectors.reshape(span, count, HEADS, HEAD_DIM)
    scores = jnp.einsum("thd,jthd->jht", query_heads, key_heads, preferred_element_type=jnp.float32)
    scores = scores * (temper / math.sqrt(HEAD_DIM))[None, :, None]
    top = jnp.max(jnp.where(permitted_mask, scores, -jnp.inf), axis=0, keepdims=True)
    weights = jnp.where(permitted_mask, jnp.exp(scores - top), 0.0)
    probs = (weights / jnp.sum(weights, axis=0, keepdims=True)).astype(jnp.bfloat16)
    combined_result_field = jnp.einsum(
        "jht,jthd->thd", probs, value_heads, preferred_element_type=jnp.float32
    )
    return combined_result_field.reshape(count, token_extent).astype(jnp.bfloat16)


def body(
    noisy_snapshot_stack,
    gaussian_perturbation,
    snapshot_noise_indices,
    partition_longitude_starts,
    latitude_patch_tally,
    normalizer_scaling,
    head_score_scales,
    local_projection_matrices,
    time_projection_matrices,
    final_projection_matrices,
):
    frames, rows, lon, token_extent = noisy_snapshot_stack.shape
    token_grid = frames * rows * lon
    band = lax.axis_index("band")
    frame_base = lax.axis_index("frame") * frames
    total_levels = lax.axis_size("frame") * frames
    state_f = noisy_snapshot_stack.astype(jnp.float32)
    normed = (
        state_f
        * lax.rsqrt(jnp.mean(state_f * state_f, axis=-1, keepdims=True) + epsilon)
        * normalizer_scaling
    ).astype(jnp.bfloat16)
    margin = 0
    space_rows = normed.reshape(-1, token_extent)
    space_proj = jnp.dot(
        space_rows,
        lax.all_gather(local_projection_matrices, "band", axis=1, tiled=True),
        preferred_element_type=jnp.float32,
    )
    space_proj = space_proj.reshape(frames, rows + 2 * margin, lon, 3 * token_extent)
    window_queries = unit_heads(space_proj[:, margin : margin + rows, :, :token_extent]).astype(
        jnp.bfloat16
    )
    space_key = unit_heads(space_proj[..., token_extent : 2 * token_extent]).astype(jnp.bfloat16)
    space_value = space_proj[..., 2 * token_extent :].astype(jnp.bfloat16)
    stacked = extended(jnp.stack([space_key, space_value]), (("band", 2),), 1)
    fringe_lookup_vectors = stacked[0]
    fringe_content_vectors = stacked[1]
    plane = rows * lon
    time_rows = normed.reshape(-1, token_extent)
    time_proj = jnp.dot(
        time_rows,
        lax.all_gather(time_projection_matrices, "band", axis=1, tiled=True),
        preferred_element_type=jnp.float32,
    )
    span = PRIOR_SNAPSHOTS + 1
    time_proj = time_proj.reshape(normed.shape[0], rows, lon, 3 * token_extent)
    temporal_queries = unit_heads(time_proj[-frames:, :, :, :token_extent]).astype(jnp.bfloat16)
    time_key = unit_heads(time_proj[..., token_extent : 2 * token_extent]).astype(jnp.bfloat16)
    time_value = time_proj[..., 2 * token_extent :].astype(jnp.bfloat16)

    def shift_values(block, hop):
        return shifted(block, "frame", hop)

    joined = with_past(jnp.stack([time_key, time_value]), 1, shift_values)
    keys_all = joined[0]
    values_all = joined[1]
    key_columns = jnp.stack([keys_all[j : j + frames] for j in range(span)]).reshape(
        span, token_grid, token_extent
    )
    value_columns = jnp.stack([values_all[j : j + frames] for j in range(span)]).reshape(
        span, token_grid, token_extent
    )
    frame_of = jnp.arange(token_grid) // plane
    position = frame_base + frame_of[None, :] - PRIOR_SNAPSHOTS + jnp.arange(span)[:, None]
    permitted_mask = (position >= 0)[:, None, :]
    time_mix = across_time_mixer(
        temporal_queries.reshape(token_grid, token_extent),
        key_columns,
        value_columns,
        permitted_mask,
        head_score_scales[1],
    )
    inner = jnp.arange(rows)[:, None] * lon + jnp.arange(lon)[None, :]
    own_valid = inner < pick(latitude_patch_tally, band)
    above = inner < pick(latitude_patch_tally, band - 1)
    below = inner < pick(latitude_patch_tally, band + 1)
    fringe_present_flags = jnp.concatenate([above, own_valid, below], axis=0)
    space_parts = [
        local_patch_mixer(
            window_queries[0],
            fringe_lookup_vectors[0],
            fringe_content_vectors[0],
            fringe_present_flags,
            partition_longitude_starts[0],
            head_score_scales[0],
        )
    ]
    space_mix = jnp.stack(space_parts).reshape(token_grid, token_extent)
    mixed = jnp.concatenate([space_mix, time_mix], axis=1)
    update = jnp.dot(
        mixed,
        lax.all_gather(final_projection_matrices, "band", axis=1, tiled=True),
        preferred_element_type=jnp.float32,
    ).reshape(frames, rows, lon, token_extent)
    sigma = sigma_of(snapshot_noise_indices, total_levels)[:, None, None, None]
    sigma_next = sigma_of(snapshot_noise_indices - 1, total_levels)[:, None, None, None]
    denoised = state_f / (1.0 + sigma * sigma) + sigma * lax.rsqrt(1.0 + sigma * sigma) * update
    noise_f = gaussian_perturbation.astype(jnp.float32)
    stepped = denoised + sigma_next * (
        keep_share * (state_f - denoised) / sigma + fresh_share * noise_f
    )
    finished = (snapshot_noise_indices == 0)[:, None, None, None]
    return jnp.where(finished, sigma_high * noise_f, stepped).astype(jnp.bfloat16)


def solution(mesh):
    return jax.shard_map(
        body,
        mesh=mesh,
        in_specs=(
            P("frame", "band", None, None),
            P("frame", "band", None, None),
            P("frame"),
            P("frame"),
            P(),
            P(),
            P(),
            P(None, "band"),
            P(None, "band"),
            P(None, "band"),
        ),
        out_specs=P("frame", "band", None, None),
        check_vma=False,
    )
```

profile of v0, /device:TPU:0, one launch (start us, length us, event | category | flops | bytes accessed | tf_op | source)
XLA Modules:
  0.0 159.1 jit_solution(10543922075528884963)
XLA Ops:
  6.5 0.7 all-gather.4.cloned.1.call-update
  7.3 0.7 all-gather.6.cloned.1.call-update
  9.4 1.0 fusion.24
  10.5 0.8 multiply_bitcast_fusion.1
  11.3 1.4 fusion.55
  13.3 1.3 iota_compare_fusion.2
  16.0 40.5 %all-gather.4.cloned.1.call-done = bf16[512,1536]{0,1:T(8,128)(2,1)} async-done(((bf16[512,192]{0,1:T(8,128)(2,1)}), bf16[512,1536]{0,1:T(8,128)(2,1)}) %all-gather.4.cloned.1.call-update) | async-done | bytes 1572880 | tf_op jit(solution)/shard_map/all_gather | solution.py:159
  56.5 2.2 %convolution_bitcast_fusion.1 = f32[1,1,180,1536]{3,2,1,0:T(8,128)S(1)} fusion(bf16[512,1536]{0,1:T(8,128)(2,1)} %all-gather.4.cloned.1.call-done, bf16[1,1,180,512]{3,2,1,0:T(8,128)(2,1)} %param.12, f32[512]{0:T(512)} %param.17, f32[180]{0:T(256)S(1)} %add_rsqrt_fusion.4), kind=kOutput, calls=%fused_computation.2 | convolution fusion | flops 283484160 | bytes 2865872 | tf_op jit(solution)/shard_map/dot_general | solution.py:157
  59.8 0.8 fusion.36
  60.6 0.8 pad_maximum_fusion.1
  61.4 3.2 %collective-permute-start = (bf16[2,1,1,180,512]{4,3,2,1,0:T(8,128)(2,1)}, bf16[2,1,1,180,512]{4,3,2,1,0:T(8,128)(2,1)}, u32[]{:S(2)}, u32[]{:S(2)}) collective-permute-start(bf16[2,1,1,180,512]{4,3,2,1,0:T(8,128)(2,1)} %pad_maximum_fusion.1), channel_id=1, source_target_pairs={{0,1},{1,2},{2,3},{3,4},{4,5},{5,6},{6,7},{8,9},{9,10},{10,11},{11... | collective-permute-start | bytes 1105928 | tf_op jit(solution)/shard_map/ppermute | solution.py:26
  64.6 1.3 collective-permute-start.1
  65.9 43.0 %all-gather.6.cloned.1.call-done = bf16[512,1536]{0,1:T(8,128)(2,1)} async-done(((bf16[512,192]{0,1:T(8,128)(2,1)}), bf16[512,1536]{0,1:T(8,128)(2,1)}) %all-gather.6.cloned.1.call-update) | async-done | bytes 1572880 | tf_op jit(solution)/shard_map/all_gather | solution.py:175
  108.8 2.1 %convolution_bitcast_fusion = f32[1,1,180,1536]{3,2,1,0:T(8,128)S(1)} fusion(bf16[512,1536]{0,1:T(8,128)(2,1)} %all-gather.6.cloned.1.call-done, bf16[1,1,180,512]{3,2,1,0:T(8,128)(2,1)S(1)} %copy-done, f32[512]{0:T(512)S(1)} %copy-done.4, f32[180]{0:T(256)S(1)} %add_rsqrt_fusion.4), kind=kOutput, calls=%fused_computation.1 | convolution fusion | flops 283484160 | bytes 2865872 | tf_op jit(solution)/shard_map/dot_general | solution.py:173
  112.2 0.8 pad_maximum_fusion.2
  113.0 2.9 %collective-permute-start.2 = (bf16[2,1,1,180,512]{4,3,2,1,0:T(8,128)(2,1)}, bf16[2,1,1,180,512]{4,3,2,1,0:T(8,128)(2,1)}, u32[]{:S(2)}, u32[]{:S(2)}) collective-permute-start(bf16[2,1,1,180,512]{4,3,2,1,0:T(8,128)(2,1)} %pad_maximum_fusion.2), channel_id=1, source_target_pairs={{0,24},{1,25},{2,26},{3,27},{4,28},{5,29},{6,30},{7,31}} | collective-permute-start | bytes 1105928 | tf_op jit(solution)/shard_map/ppermute | solution.py:38
  115.9 2.6 %collective-permute-start.3 = (bf16[2,1,1,180,512]{4,3,2,1,0:T(8,128)(2,1)}, bf16[2,1,1,180,512]{4,3,2,1,0:T(8,128)(2,1)}, u32[]{:S(2)}, u32[]{:S(2)}) collective-permute-start(bf16[2,1,1,180,512]{4,3,2,1,0:T(8,128)(2,1)} %pad_maximum_fusion.2), channel_id=1, source_target_pairs={{0,16},{8,24},{1,17},{9,25},{2,18},{10,26},{3,19},{11,27},{4,20},{... | collective-permute-start | bytes 1105928 | tf_op jit(solution)/shard_map/ppermute | solution.py:38
  118.5 2.0 %collective-permute-start.4 = (bf16[2,1,1,180,512]{4,3,2,1,0:T(8,128)(2,1)}, bf16[2,1,1,180,512]{4,3,2,1,0:T(8,128)(2,1)}, u32[]{:S(2)}, u32[]{:S(2)}) collective-permute-start(bf16[2,1,1,180,512]{4,3,2,1,0:T(8,128)(2,1)} %pad_maximum_fusion.2), channel_id=1, source_target_pairs={{0,8},{8,16},{16,24},{1,9},{9,17},{17,25},{2,10},{10,18},{18,26},{... | collective-permute-start | bytes 1105928 | tf_op jit(solution)/shard_map/ppermute | solution.py:38
  121.5 0.8 copy.67
  122.3 1.2 pad_maximum_fusion
  123.7 1.2 fusion.16
  126.6 0.8 convolution_multiply_fusion
  127.3 1.7 %fusion.67 = (f32[3,8,60]{2,1,0:T(8,128)S(1)}, f32[3,8,60,180]{3,2,1,0:T(8,128)}) fusion(f32[3,8,60,180]{3,2,1,0:T(8,128)S(1)} %convolution_multiply_fusion, pred[3,60,180]{2,1,0:T(8,128)(4,1)S(1)} %broadcast_or_fusion), kind=kOutput, calls=%fused_computation.140 | output fusion | flops 1036979 | bytes 2111760 | tf_op jit(solution)/shard_map/sub | solution.py:106
  129.3 1.1 copy.45
  130.5 1.1 copy.46
  132.1 2.7 %convolution_bitcast_fusion.2 = bf16[1,3,60,8,64]{2,4,3,1,0:T(8,128)(2,1)} fusion(bf16[1,3,60,8,64]{2,4,3,1,0:T(8,128)(2,1)S(1)} %copy.47, bf16[1,3,60,8,64]{2,4,3,1,0:T(8,128)(2,1)} %copy.46, bf16[1,3,60,8,64]{2,4,3,1,0:T(8,128)(2,1)} %copy.45, f32[3,8,60,180]{3,2,1,0:T(8,128)S(1)} %copy-done.1, f32[3,8,60]{2,1,0:T(8,128)S(1)} %get-tuple-element.36), kind=kOutput, calls=%fused_computation.10 | convolution fusion | flops 35354880 | bytes 1779840 | tf_op jit(solution)/shard_map/rwhqk,rwkhd->rwqhd/dot_general | solution.py:108
  134.8 1.3 copy.54
  136.3 1.0 fusion.64
  137.5 1.0 fusion.65
  138.7 1.1 fusion.66
  141.8 8.2 %all-gather.8.cloned.1.call-done = bf16[1024,512]{0,1:T(8,128)(2,1)} async-done(((bf16[1024,64]{0,1:T(8,128)(2,1)}), bf16[1024,512]{0,1:T(8,128)(2,1)}) %all-gather.8.cloned.1.call-update) | async-done | bytes 1048592 | tf_op jit(solution)/shard_map/all_gather | solution.py:225
  150.0 2.5 %fusion.20 = bf16[1,1,180,512]{3,2,1,0:T(8,128)(2,1)} fusion(bf16[1,1,180,512]{3,2,1,0:T(8,128)(2,1)S(1)} %copy-done.5, bf16[1,1,180,512]{3,2,1,0:T(8,128)(2,1)S(1)} %copy-done, bf16[1024,512]{0,1:T(8,128)(2,1)} %all-gather.8.cloned.1.call-done, bf16[180,512]{1,0:T(8,128)(2,1)S(1)} %copy.68, bf16[180,512]{1,0:T(8,128)(2,1)S(1)} %fusion.38, f32[]{:T(128)} %bitcast.51, ...), kind=kOutput, calls=%fused_computation.47 | convolution fusion | flops 190863360 | bytes 1970193 | tf_op jit(solution)/shard_map/dot_general | solution.py:223
  (92 shorter events, 10.3 us)
Async XLA Ops:
  6.5 49.9 %all-gather.4.cloned.1.call-start = ((), (), s32[]{:S(2)}) async-start(), calls=%async_computation | async-start | bytes 1769472 | tf_op jit(solution)/shard_map/all_gather | solution.py:159
  7.3 101.6 %all-gather.6.cloned.1.call-start = ((), (), s32[]{:S(2)}) async-start(), calls=%async_computation.1 | async-start | bytes 1769472 | tf_op jit(solution)/shard_map/all_gather | solution.py:175
  8.0 142.0 %all-gather.8.cloned.1.call-start = ((), (), s32[]{:S(2)}) async-start(), calls=%async_computation.2 | async-start | bytes 1179648 | tf_op jit(solution)/shard_map/all_gather | solution.py:225
  59.6 49.2 %copy-start = (bf16[1,1,180,512]{3,2,1,0:T(8,128)(2,1)S(1)}, bf16[1,1,180,512]{3,2,1,0:T(8,128)(2,1)}, u32[]{:S(2)}) copy-start(bf16[1,1,180,512]{3,2,1,0:T(8,128)(2,1)} %param.12) | copy-start | bytes 552964
  59.6 49.2 %copy-start.4 = (f32[512]{0:T(512)S(1)}, f32[512]{0:T(512)}, u32[]{:S(2)}) copy-start(f32[512]{0:T(512)} %param.17) | copy-start | bytes 6148
  61.4 61.0 %collective-permute-start = (bf16[2,1,1,180,512]{4,3,2,1,0:T(8,128)(2,1)}, bf16[2,1,1,180,512]{4,3,2,1,0:T(8,128)(2,1)}, u32[]{:S(2)}, u32[]{:S(2)}) collective-permute-start(bf16[2,1,1,180,512]{4,3,2,1,0:T(8,128)(2,1)} %pad_maximum_fusion.1), channel_id=1, source_target_pairs={{0,1},{1,2},{2,3},{3,4},{4,5},{5,6},{6,7},{8,9},{9,10},{10,11},{11... | collective-permute-start | bytes 1105928 | tf_op jit(solution)/shard_map/ppermute | solution.py:26
  64.6 57.8 %collective-permute-start.1 = (bf16[2,1,1,180,512]{4,3,2,1,0:T(8,128)(2,1)}, bf16[2,1,1,180,512]{4,3,2,1,0:T(8,128)(2,1)}, u32[]{:S(2)}, u32[]{:S(2)}) collective-permute-start(bf16[2,1,1,180,512]{4,3,2,1,0:T(8,128)(2,1)} %pad_maximum_fusion.1), channel_id=1, source_target_pairs={{1,0},{2,1},{3,2},{4,3},{5,4},{6,5},{7,6},{9,8},{10,9},{11,10},{12... | collective-permute-start | bytes 1105928 | tf_op jit(solution)/shard_map/ppermute | solution.py:28
  112.0 8.7 %copy-start.3 = (bf16[1,180,512]{2,1,0:T(8,128)(2,1)S(1)}, bf16[1,180,512]{2,1,0:T(8,128)(2,1)}, u32[]{:S(2)}) copy-start(bf16[1,180,512]{2,1,0:T(8,128)(2,1)} %get-tuple-element.12) | copy-start | bytes 552964
  113.0 23.3 %collective-permute-start.2 = (bf16[2,1,1,180,512]{4,3,2,1,0:T(8,128)(2,1)}, bf16[2,1,1,180,512]{4,3,2,1,0:T(8,128)(2,1)}, u32[]{:S(2)}, u32[]{:S(2)}) collective-permute-start(bf16[2,1,1,180,512]{4,3,2,1,0:T(8,128)(2,1)} %pad_maximum_fusion.2), channel_id=1, source_target_pairs={{0,24},{1,25},{2,26},{3,27},{4,28},{5,29},{6,30},{7,31}} | collective-permute-start | bytes 1105928 | tf_op jit(solution)/shard_map/ppermute | solution.py:38
  115.9 21.6 %collective-permute-start.3 = (bf16[2,1,1,180,512]{4,3,2,1,0:T(8,128)(2,1)}, bf16[2,1,1,180,512]{4,3,2,1,0:T(8,128)(2,1)}, u32[]{:S(2)}, u32[]{:S(2)}) collective-permute-start(bf16[2,1,1,180,512]{4,3,2,1,0:T(8,128)(2,1)} %pad_maximum_fusion.2), channel_id=1, source_target_pairs={{0,16},{8,24},{1,17},{9,25},{2,18},{10,26},{3,19},{11,27},{4,20},{... | collective-permute-start | bytes 1105928 | tf_op jit(solution)/shard_map/ppermute | solution.py:38
  118.5 20.2 %collective-permute-start.4 = (bf16[2,1,1,180,512]{4,3,2,1,0:T(8,128)(2,1)}, bf16[2,1,1,180,512]{4,3,2,1,0:T(8,128)(2,1)}, u32[]{:S(2)}, u32[]{:S(2)}) collective-permute-start(bf16[2,1,1,180,512]{4,3,2,1,0:T(8,128)(2,1)} %pad_maximum_fusion.2), channel_id=1, source_target_pairs={{0,8},{8,16},{16,24},{1,9},{9,17},{17,25},{2,10},{10,18},{18,26},{... | collective-permute-start | bytes 1105928 | tf_op jit(solution)/shard_map/ppermute | solution.py:38
  129.2 2.9 %copy-start.1 = (f32[3,8,60,180]{3,2,1,0:T(8,128)S(1)}, f32[3,8,60,180]{3,2,1,0:T(8,128)}, u32[]{:S(2)}) copy-start(f32[3,8,60,180]{3,2,1,0:T(8,128)} %get-tuple-element.37) | copy-start | bytes 3110404
  139.9 1.0 copy-start.2
  140.7 9.3 %copy-start.5 = (bf16[1,1,180,512]{3,2,1,0:T(8,128)(2,1)S(1)}, bf16[1,1,180,512]{3,2,1,0:T(8,128)(2,1)}, u32[]{:S(2)}) copy-start(bf16[1,1,180,512]{3,2,1,0:T(8,128)(2,1)} %param.13) | copy-start | bytes 552964
Sparse Core Ops, SparseCore 0:
  9.5 46.8 all-gather.3
  58.6 50.1 all-gather.5
  111.0 39.0 all-gather.7
where the time goes:
time: 160 us; the launch traced here: 159 us
  waiting for transfers between devices  93.8 us (59%)
  between operations  15.2 us (10%)
  other arithmetic  14 us (9%)
  local copies, waits for them, and re-layouts  13.8 us (9%)
  starting transfers between devices  12.1 us (8%)
  matrix products  10.2 us (6%)
    all_gather x1, waiting for transfers between devices, body(): lax.all_gather(time_projection_matrices, 'band', axis=1, tiled=True)  43 us
    all_gather x1, waiting for transfers between devices, body(): lax.all_gather(local_projection_matrices, 'band', axis=1, tiled=True)  40.5 us
    all_gather x1, waiting for transfers between devices, body(): lax.all_gather(final_projection_matrices, 'band', axis=1, tiled=True)  8.25 us
    ppermute x3, starting transfers between devices, shifted(): return lax.ppermute(block, axis, route)  7.54 us
    slice x6, local copies, waits for them, and re-layouts, body(): keys_all[j:j + frames]  3.53 us
  transfers between devices with their start and end apart: 8, of which 3 were waited for; matrix products, arithmetic and copies ran while one was open for 22% of the time, Pallas kernels for 0%

commit v1 on v0

--- a/solution.py
+++ b/solution.py
@@ -13,6 +13,23 @@
 sigma_high = 2.0
 keep_share = 0.8
 fresh_share = 0.6
+
+
+def laid_out(blocks, dim):
+    blocks = jnp.moveaxis(blocks, 0, dim)
+    shape = blocks.shape
+    return blocks.reshape(*shape[:dim], shape[dim] * shape[dim + 1], *shape[dim + 2 :])
+
+
+def collect(x, axis, dim):
+    size = lax.axis_size(axis)
+    upward = [(i, (i + 1) % size) for i in range(size)]
+    tiles = [x]
+    while len(tiles) < size:
+        tiles.append(lax.ppermute(tiles[-1], axis, upward))
+    place = lax.axis_index(axis)
+    tiles = jnp.stack(tiles)[(place - jnp.arange(size)) % size]
+    return laid_out(tiles, dim)
 
 
 def extended(cells, sides, width):
@@ -156,7 +173,7 @@
     space_rows = normed.reshape(-1, token_extent)
     space_proj = jnp.dot(
         space_rows,
-        lax.all_gather(local_projection_matrices, "band", axis=1, tiled=True),
+        collect(local_projection_matrices, "band", 1),
         preferred_element_type=jnp.float32,
     )
     space_proj = space_proj.reshape(frames, rows + 2 * margin, lon, 3 * token_extent)

time: 160 us -> 147 us (0.919)
  the two profiles are of different devices: /device:TPU:0 before, /device:TPU:18 now
where the time goes in v1:
time: 147 us
  waiting for transfers between devices  75.5 us (51%)
  local copies, waits for them, and re-layouts  19.9 us (14%)
  between operations  15.6 us (11%)
  starting transfers between devices  15.4 us (10%)
  other arithmetic  12.7 us (9%)
  matrix products  7.59 us (5%)
    ppermute x7, waiting for transfers between devices, collect(): tiles.append(lax.ppermute(tiles[-1], axis, upward))  51.9 us
    ppermute x1, waiting for transfers between devices, extended(): lax.ppermute(tail, axis, [(i, (i + 1) % count) for i in range(ends)])  9.7 us
    ppermute x3, waiting for transfers between devices, shifted(): return lax.ppermute(block, axis, route)  7.36 us
    ppermute x1, waiting for transfers between devices, extended(): lax.ppermute(head, axis, [((i + 1) % count, i) for i in range(ends)])  5.77 us
    ppermute x1, starting transfers between devices, extended(): lax.ppermute(head, axis, [((i + 1) % count, i) for i in range(ends)])  4.82 us
    ppermute x3, starting transfers between devices, shifted(): return lax.ppermute(block, axis, route)  4.8 us
    ppermute x7, starting transfers between devices, collect(): tiles.append(lax.ppermute(tiles[-1], axis, upward))  3.78 us
    slice x6, local copies, waits for them, and re-layouts, body(): keys_all[j:j + frames]  3.52 us
  transfers between devices with their start and end apart: 14, of which 9 were waited for; matrix products, arithmetic and copies ran while one was open for 25% of the time, Pallas kernels for 0%

profile of v1, /device:TPU:18, one launch (start us, length us, event | category | flops | bytes accessed | tf_op | source)
XLA Modules:
  0.0 146.6 jit_solution(3433694857812090252)
XLA Ops:
  7.3 1.6 %collective-permute-start = (bf16[512,192]{0,1:T(8,128)(2,1)}, bf16[512,192]{0,1:T(8,128)(2,1)S(1)}, u32[]{:S(2)}, u32[]{:S(2)}) collective-permute-start(bf16[512,192]{0,1:T(8,128)(2,1)} %param.19), channel_id=1, source_target_pairs={{0,1},{1,2},{2,3},{3,4},{4,5},{5,6},{6,7},{7,0},{8,9},{9,10},{10,1... | collective-permute-start | bytes 589832 | tf_op jit(solution)/shard_map/ppermute | solution.py:29
  10.6 1.0 fusion.24
  12.4 1.4 fusion.55
  14.5 1.3 iota_compare_fusion.2
  16.2 1.6 %collective-permute-start.1 = (bf16[512,192]{0,1:T(8,128)(2,1)S(1)}, bf16[512,192]{0,1:T(8,128)(2,1)S(1)}, u32[]{:S(2)}, u32[]{:S(2)}) collective-permute-start(bf16[512,192]{0,1:T(8,128)(2,1)S(1)} %collective-permute-done), channel_id=1, source_target_pairs={{0,1},{1,2},{2,3},{3,4},{4,5},{5,6},{6,7},{7,0},{8,9},{9,10},{10,1... | collective-permute-start | bytes 589832 | tf_op jit(solution)/shard_map/ppermute | solution.py:29
  17.8 8.0 %collective-permute-done.1 = bf16[512,192]{0,1:T(8,128)(2,1)S(1)} collective-permute-done((bf16[512,192]{0,1:T(8,128)(2,1)S(1)}, bf16[512,192]{0,1:T(8,128)(2,1)S(1)}, u32[]{:S(2)}, u32[]{:S(2)}) %collective-permute-start.1) | collective-permute-done | bytes 196640 | tf_op jit(solution)/shard_map/ppermute | solution.py:29
  26.4 8.4 %collective-permute-done.2 = bf16[512,192]{0,1:T(8,128)(2,1)S(1)} collective-permute-done((bf16[512,192]{0,1:T(8,128)(2,1)S(1)}, bf16[512,192]{0,1:T(8,128)(2,1)S(1)}, u32[]{:S(2)}, u32[]{:S(2)}) %collective-permute-start.2) | collective-permute-done | bytes 196640 | tf_op jit(solution)/shard_map/ppermute | solution.py:29
  34.8 6.5 %collective-permute-done.3 = bf16[512,192]{0,1:T(8,128)(2,1)S(1)} collective-permute-done((bf16[512,192]{0,1:T(8,128)(2,1)S(1)}, bf16[512,192]{0,1:T(8,128)(2,1)S(1)}, u32[]{:S(2)}, u32[]{:S(2)}) %collective-permute-start.3) | collective-permute-done | bytes 196640 | tf_op jit(solution)/shard_map/ppermute | solution.py:29
  41.4 12.6 %collective-permute-done.4 = bf16[512,192]{0,1:T(8,128)(2,1)S(1)} collective-permute-done((bf16[512,192]{0,1:T(8,128)(2,1)S(1)}, bf16[512,192]{0,1:T(8,128)(2,1)S(1)}, u32[]{:S(2)}, u32[]{:S(2)}) %collective-permute-start.4) | collective-permute-done | bytes 196640 | tf_op jit(solution)/shard_map/ppermute | solution.py:29
  54.0 9.2 %collective-permute-done.5 = bf16[512,192]{0,1:T(8,128)(2,1)S(1)} collective-permute-done((bf16[512,192]{0,1:T(8,128)(2,1)S(1)}, bf16[512,192]{0,1:T(8,128)(2,1)S(1)}, u32[]{:S(2)}, u32[]{:S(2)}) %collective-permute-start.5) | collective-permute-done | bytes 196640 | tf_op jit(solution)/shard_map/ppermute | solution.py:29
  63.2 7.2 %collective-permute-done.6 = bf16[512,192]{0,1:T(8,128)(2,1)S(1)} collective-permute-done((bf16[512,192]{0,1:T(8,128)(2,1)S(1)}, bf16[512,192]{0,1:T(8,128)(2,1)S(1)}, u32[]{:S(2)}, u32[]{:S(2)}) %collective-permute-start.6) | collective-permute-done | bytes 196640 | tf_op jit(solution)/shard_map/ppermute | solution.py:29
  73.4 1.9 %collective-permute-start.7 = (bf16[2,1,1,180,512]{4,3,2,1,0:T(8,128)(2,1)S(1)}, bf16[2,1,1,180,512]{4,3,2,1,0:T(8,128)(2,1)S(1)}, u32[]{:S(2)}, u32[]{:S(2)}) collective-permute-start(bf16[2,1,1,180,512]{4,3,2,1,0:T(8,128)(2,1)S(1)} %pad_maximum_fusion.1), channel_id=1, source_target_pairs={{0,1},{1,2},{2,3},{3,4},{4,5},{5,6},{6,7},{8,9},{9,10},{10,11},{11... | collective-permute-start | bytes 1105928 | tf_op jit(solution)/shard_map/ppermute | solution.py:43
  75.3 4.8 %collective-permute-start.8 = (bf16[2,1,1,180,512]{4,3,2,1,0:T(8,128)(2,1)S(1)}, bf16[2,1,1,180,512]{4,3,2,1,0:T(8,128)(2,1)S(1)}, u32[]{:S(2)}, u32[]{:S(2)}) collective-permute-start(bf16[2,1,1,180,512]{4,3,2,1,0:T(8,128)(2,1)S(1)} %pad_maximum_fusion.1), channel_id=1, source_target_pairs={{1,0},{2,1},{3,2},{4,3},{5,4},{6,5},{7,6},{9,8},{10,9},{11,10},{12... | collective-permute-start | bytes 1105928 | tf_op jit(solution)/shard_map/ppermute | solution.py:45
  81.7 9.7 %collective-permute-done.7 = bf16[2,1,1,180,512]{4,3,2,1,0:T(8,128)(2,1)S(1)} collective-permute-done((bf16[2,1,1,180,512]{4,3,2,1,0:T(8,128)(2,1)S(1)}, bf16[2,1,1,180,512]{4,3,2,1,0:T(8,128)(2,1)S(1)}, u32[]{:S(2)}, u32[]{:S(2)}) %collective-permute-start.7) | collective-permute-done | bytes 368672 | tf_op jit(solution)/shard_map/ppermute | solution.py:43
  91.4 5.8 %collective-permute-done.8 = bf16[2,1,1,180,512]{4,3,2,1,0:T(8,128)(2,1)S(1)} collective-permute-done((bf16[2,1,1,180,512]{4,3,2,1,0:T(8,128)(2,1)S(1)}, bf16[2,1,1,180,512]{4,3,2,1,0:T(8,128)(2,1)S(1)}, u32[]{:S(2)}, u32[]{:S(2)}) %collective-permute-start.8) | collective-permute-done | bytes 368672 | tf_op jit(solution)/shard_map/ppermute | solution.py:45
  97.4 1.2 fusion.16
  100.5 1.1 copy.45
  101.8 1.1 copy.46
  103.1 1.0 copy.47
  105.7 2.1 %convolution_bitcast_fusion = f32[1,1,180,1536]{3,2,1,0:T(8,128)S(1)} fusion(bf16[512,1536]{0,1:T(8,128)(2,1)} %all-gather.3.cloned.1.call-done, bf16[1,1,180,512]{3,2,1,0:T(8,128)(2,1)S(1)} %copy-done, f32[512]{0:T(512)S(1)} %copy-done.5, f32[180]{0:T(256)S(1)} %add_rsqrt_fusion.4), kind=kOutput, calls=%fused_computation.2 | convolution fusion | flops 283484160 | bytes 2865872 | tf_op jit(solution)/shard_map/dot_general | solution.py:190
  109.4 1.2 copy.55
  111.6 1.2 copy.61
  113.9 1.3 multiply_convert_fusion
  116.0 1.4 collective-permute-start.9
  117.5 1.5 collective-permute-start.10
  118.9 1.5 %convolution_bitcast_fusion.2 = bf16[1,3,60,8,64]{2,4,3,1,0:T(8,128)(2,1)} fusion(bf16[1,3,60,8,64]{2,4,3,1,0:T(8,128)(2,1)S(1)} %copy-done.4, bf16[1,3,60,8,64]{2,4,3,1,0:T(8,128)(2,1)S(1)} %copy-done.3, bf16[1,3,60,8,64]{2,4,3,1,0:T(8,128)(2,1)S(1)} %copy-done.2, f32[3,8,60,180]{3,2,1,0:T(8,128)S(1)} %get-tuple-element.37, ...), kind=kOutput, calls=%fused_computation.11 | convolution fusion | flops 35354880 | bytes 1779840 | tf_op jit(solution)/shard_map/rwhqk,rwkhd->rwqhd/dot_general | solution.py:125
  120.5 1.3 copy.54
  122.4 1.9 %collective-permute-start.11 = (bf16[2,1,1,180,512]{4,3,2,1,0:T(8,128)(2,1)}, bf16[2,1,1,180,512]{4,3,2,1,0:T(8,128)(2,1)}, u32[]{:S(2)}, u32[]{:S(2)}) collective-permute-start(bf16[2,1,1,180,512]{4,3,2,1,0:T(8,128)(2,1)} %pad_maximum_fusion.2), channel_id=1, source_target_pairs={{0,8},{8,16},{16,24},{1,9},{9,17},{17,25},{2,10},{10,18},{18,26},{... | collective-permute-start | bytes 1105928 | tf_op jit(solution)/shard_map/ppermute | solution.py:55
  124.8 1.0 fusion.66
  126.0 7.3 %collective-permute-done.10 = bf16[2,1,1,180,512]{4,3,2,1,0:T(8,128)(2,1)} collective-permute-done((bf16[2,1,1,180,512]{4,3,2,1,0:T(8,128)(2,1)}, bf16[2,1,1,180,512]{4,3,2,1,0:T(8,128)(2,1)}, u32[]{:S(2)}, u32[]{:S(2)}) %collective-permute-start.10) | collective-permute-done | bytes 368672 | tf_op jit(solution)/shard_map/ppermute | solution.py:55
  134.6 1.0 fusion.68
  137.2 2.5 %fusion.20 = bf16[1,1,180,512]{3,2,1,0:T(8,128)(2,1)} fusion(bf16[1,1,180,512]{3,2,1,0:T(8,128)(2,1)S(1)} %copy-done.6, bf16[1,1,180,512]{3,2,1,0:T(8,128)(2,1)S(1)} %copy-done, bf16[1024,512]{0,1:T(8,128)(2,1)} %all-gather.5.cloned.1.call-done, bf16[180,512]{1,0:T(8,128)(2,1)S(1)} %copy.68, bf16[180,512]{1,0:T(8,128)(2,1)S(1)} %fusion.38, f32[]{:T(128)} %bitcast.62, ...), kind=kOutput, calls=%fused_computation.48 | convolution fusion | flops 190863360 | bytes 1970193 | tf_op jit(solution)/shard_map/dot_general | solution.py:240
  (116 shorter events, 20.4 us)
Async XLA Ops:
  6.5 99.2 %all-gather.3.cloned.1.call-start = ((), (), s32[]{:S(2)}) async-start(), calls=%async_computation | async-start | bytes 1769472 | tf_op jit(solution)/shard_map/all_gather | solution.py:192
  7.3 130.0 %all-gather.5.cloned.1.call-start = ((), (), s32[]{:S(2)}) async-start(), calls=%async_computation.1 | async-start | bytes 1179648 | tf_op jit(solution)/shard_map/all_gather | solution.py:242
  7.3 8.9 %collective-permute-start = (bf16[512,192]{0,1:T(8,128)(2,1)}, bf16[512,192]{0,1:T(8,128)(2,1)S(1)}, u32[]{:S(2)}, u32[]{:S(2)}) collective-permute-start(bf16[512,192]{0,1:T(8,128)(2,1)} %param.19), channel_id=1, source_target_pairs={{0,1},{1,2},{2,3},{3,4},{4,5},{5,6},{6,7},{7,0},{8,9},{9,10},{10,1... | collective-permute-start | bytes 589832 | tf_op jit(solution)/shard_map/ppermute | solution.py:29
  16.2 9.6 %collective-permute-start.1 = (bf16[512,192]{0,1:T(8,128)(2,1)S(1)}, bf16[512,192]{0,1:T(8,128)(2,1)S(1)}, u32[]{:S(2)}, u32[]{:S(2)}) collective-permute-start(bf16[512,192]{0,1:T(8,128)(2,1)S(1)} %collective-permute-done), channel_id=1, source_target_pairs={{0,1},{1,2},{2,3},{3,4},{4,5},{5,6},{6,7},{7,0},{8,9},{9,10},{10,1... | collective-permute-start | bytes 589832 | tf_op jit(solution)/shard_map/ppermute | solution.py:29
  25.8 9.0 %collective-permute-start.2 = (bf16[512,192]{0,1:T(8,128)(2,1)S(1)}, bf16[512,192]{0,1:T(8,128)(2,1)S(1)}, u32[]{:S(2)}, u32[]{:S(2)}) collective-permute-start(bf16[512,192]{0,1:T(8,128)(2,1)S(1)} %collective-permute-done.1), channel_id=1, source_target_pairs={{0,1},{1,2},{2,3},{3,4},{4,5},{5,6},{6,7},{7,0},{8,9},{9,10},{10,1... | collective-permute-start | bytes 589832 | tf_op jit(solution)/shard_map/ppermute | solution.py:29
  34.8 6.6 %collective-permute-start.3 = (bf16[512,192]{0,1:T(8,128)(2,1)S(1)}, bf16[512,192]{0,1:T(8,128)(2,1)S(1)}, u32[]{:S(2)}, u32[]{:S(2)}) collective-permute-start(bf16[512,192]{0,1:T(8,128)(2,1)S(1)} %collective-permute-done.2), channel_id=1, source_target_pairs={{0,1},{1,2},{2,3},{3,4},{4,5},{5,6},{6,7},{7,0},{8,9},{9,10},{10,1... | collective-permute-start | bytes 589832 | tf_op jit(solution)/shard_map/ppermute | solution.py:29
  41.4 12.6 %collective-permute-start.4 = (bf16[512,192]{0,1:T(8,128)(2,1)S(1)}, bf16[512,192]{0,1:T(8,128)(2,1)S(1)}, u32[]{:S(2)}, u32[]{:S(2)}) collective-permute-start(bf16[512,192]{0,1:T(8,128)(2,1)S(1)} %collective-permute-done.3), channel_id=1, source_target_pairs={{0,1},{1,2},{2,3},{3,4},{4,5},{5,6},{6,7},{7,0},{8,9},{9,10},{10,1... | collective-permute-start | bytes 589832 | tf_op jit(solution)/shard_map/ppermute | solution.py:29
  54.0 9.2 %collective-permute-start.5 = (bf16[512,192]{0,1:T(8,128)(2,1)S(1)}, bf16[512,192]{0,1:T(8,128)(2,1)S(1)}, u32[]{:S(2)}, u32[]{:S(2)}) collective-permute-start(bf16[512,192]{0,1:T(8,128)(2,1)S(1)} %collective-permute-done.4), channel_id=1, source_target_pairs={{0,1},{1,2},{2,3},{3,4},{4,5},{5,6},{6,7},{7,0},{8,9},{9,10},{10,1... | collective-permute-start | bytes 589832 | tf_op jit(solution)/shard_map/ppermute | solution.py:29
  63.2 7.2 %collective-permute-start.6 = (bf16[512,192]{0,1:T(8,128)(2,1)S(1)}, bf16[512,192]{0,1:T(8,128)(2,1)S(1)}, u32[]{:S(2)}, u32[]{:S(2)}) collective-permute-start(bf16[512,192]{0,1:T(8,128)(2,1)S(1)} %collective-permute-done.5), channel_id=1, source_target_pairs={{0,1},{1,2},{2,3},{3,4},{4,5},{5,6},{6,7},{7,0},{8,9},{9,10},{10,1... | collective-permute-start | bytes 589832 | tf_op jit(solution)/shard_map/ppermute | solution.py:29
  70.5 0.9 copy-start
  70.5 0.9 copy-start.5
  73.4 17.9 %collective-permute-start.7 = (bf16[2,1,1,180,512]{4,3,2,1,0:T(8,128)(2,1)S(1)}, bf16[2,1,1,180,512]{4,3,2,1,0:T(8,128)(2,1)S(1)}, u32[]{:S(2)}, u32[]{:S(2)}) collective-permute-start(bf16[2,1,1,180,512]{4,3,2,1,0:T(8,128)(2,1)S(1)} %pad_maximum_fusion.1), channel_id=1, source_target_pairs={{0,1},{1,2},{2,3},{3,4},{4,5},{5,6},{6,7},{8,9},{9,10},{10,11},{11... | collective-permute-start | bytes 1105928 | tf_op jit(solution)/shard_map/ppermute | solution.py:43
  75.3 21.8 %collective-permute-start.8 = (bf16[2,1,1,180,512]{4,3,2,1,0:T(8,128)(2,1)S(1)}, bf16[2,1,1,180,512]{4,3,2,1,0:T(8,128)(2,1)S(1)}, u32[]{:S(2)}, u32[]{:S(2)}) collective-permute-start(bf16[2,1,1,180,512]{4,3,2,1,0:T(8,128)(2,1)S(1)} %pad_maximum_fusion.1), channel_id=1, source_target_pairs={{1,0},{2,1},{3,2},{4,3},{5,4},{6,5},{7,6},{9,8},{10,9},{11,10},{12... | collective-permute-start | bytes 1105928 | tf_op jit(solution)/shard_map/ppermute | solution.py:45
  113.9 1.4 copy-start.1
  113.9 5.0 %copy-start.2 = (bf16[1,3,60,8,64]{2,4,3,1,0:T(8,128)(2,1)S(1)}, bf16[1,3,60,8,64]{2,4,3,1,0:T(8,128)(2,1)}, u32[]{:S(2)}) copy-start(bf16[1,3,60,8,64]{2,4,3,1,0:T(8,128)(2,1)} %copy.45) | copy-start | bytes 552964
  113.9 5.1 %copy-start.3 = (bf16[1,3,60,8,64]{2,4,3,1,0:T(8,128)(2,1)S(1)}, bf16[1,3,60,8,64]{2,4,3,1,0:T(8,128)(2,1)}, u32[]{:S(2)}) copy-start(bf16[1,3,60,8,64]{2,4,3,1,0:T(8,128)(2,1)} %copy.46) | copy-start | bytes 552964
  113.9 5.1 %copy-start.4 = (bf16[1,3,60,8,64]{2,4,3,1,0:T(8,128)(2,1)S(1)}, bf16[1,3,60,8,64]{2,4,3,1,0:T(8,128)(2,1)}, u32[]{:S(2)}) copy-start(bf16[1,3,60,8,64]{2,4,3,1,0:T(8,128)(2,1)} %copy.47) | copy-start | bytes 552964
  116.0 8.8 %collective-permute-start.9 = (bf16[2,1,1,180,512]{4,3,2,1,0:T(8,128)(2,1)}, bf16[2,1,1,180,512]{4,3,2,1,0:T(8,128)(2,1)}, u32[]{:S(2)}, u32[]{:S(2)}) collective-permute-start(bf16[2,1,1,180,512]{4,3,2,1,0:T(8,128)(2,1)} %pad_maximum_fusion.2), channel_id=1, source_target_pairs={{0,24},{1,25},{2,26},{3,27},{4,28},{5,29},{6,30},{7,31}} | collective-permute-start | bytes 1105928 | tf_op jit(solution)/shard_map/ppermute | solution.py:55
  117.5 15.9 %collective-permute-start.10 = (bf16[2,1,1,180,512]{4,3,2,1,0:T(8,128)(2,1)}, bf16[2,1,1,180,512]{4,3,2,1,0:T(8,128)(2,1)}, u32[]{:S(2)}, u32[]{:S(2)}) collective-permute-start(bf16[2,1,1,180,512]{4,3,2,1,0:T(8,128)(2,1)} %pad_maximum_fusion.2), channel_id=1, source_target_pairs={{0,16},{8,24},{1,17},{9,25},{2,18},{10,26},{3,19},{11,27},{4,20},{... | collective-permute-start | bytes 1105928 | tf_op jit(solution)/shard_map/ppermute | solution.py:55
  122.4 12.2 %collective-permute-start.11 = (bf16[2,1,1,180,512]{4,3,2,1,0:T(8,128)(2,1)}, bf16[2,1,1,180,512]{4,3,2,1,0:T(8,128)(2,1)}, u32[]{:S(2)}, u32[]{:S(2)}) collective-permute-start(bf16[2,1,1,180,512]{4,3,2,1,0:T(8,128)(2,1)} %pad_maximum_fusion.2), channel_id=1, source_target_pairs={{0,8},{8,16},{16,24},{1,9},{9,17},{17,25},{2,10},{10,18},{18,26},{... | collective-permute-start | bytes 1105928 | tf_op jit(solution)/shard_map/ppermute | solution.py:55
  136.2 1.1 copy-start.6
Sparse Core Ops, SparseCore 0:
  9.5 51.6 all-gather.2
  63.4 41.5 all-gather.4
